TPU v7x, 512 devices: a whole 4x8x8 slice. The times are simulated.
512 devices in a mesh: row: 32 (over x, z), col: 16 (over y, core).
Axes of the slice: x: 4, y: 8, z: 8, core: 2. Of those that a mesh axis runs over, the one named last changes fastest.
Arguments:
- features: bfloat16 [65536, 128], P(('row', 'col')), may hold values from -6 to 6
- weight: bfloat16 [128, 256], replicated, may hold values from -0.5 to 0.5
- edge_tiles: bfloat16 [32, 16, 144, 128, 128], P('row', 'col'), may hold values from -0.046875 to 0.046875
- tile_row: int32 [32, 16, 144], P('row', 'col'), may hold values from 0 to 15
- tile_col: int32 [32, 16, 144], P('row', 'col'), may hold values from 0 to 31
- tile_count: int32 [32, 16], P('row', 'col'), may hold values from 36 to 144, as said below
- labels: int32 [65536], P(('row', 'col')), may hold values from -40 to 171
- cotangent: bfloat16 [65536, 256], P(('row', 'col')), may hold values from -6 to 6
Outputs:
- activation: bfloat16 [65536, 256], P(('row', 'col'))
- grad_features: bfloat16 [65536, 128], P(('row', 'col'))
- grad_weight: float32 [128, 256], replicated
Inputs may be any that keep to these rules, and one draw needn't show every extreme that they name: Slots 0 to tile_count[r, c] - 1 of grid block (r, c) are live and the later ones are ignored; tile positions may repeat within a block, and repeated tiles add.
All inputs are finite; a program needn't handle non-finite values.
Results may differ from a plain program's by a relative error of at most 0.029.
Values may be sent and summed in bfloat16 or wider, within the bound.
A program may use at most 64 MiB of HBM per device.

v0:
```python
import jax
import jax.numpy as jnp
from jax import lax
from jax.sharding import PartitionSpec as P

slot_group = 16


def tile_products(blocks, index_in, index_out, live_count, sources, outputs, transposed):
    groups = (live_count + slot_group - 1) // slot_group

    def advance(block_index, totals):
        offset = block_index * slot_group
        tiles_now = lax.dynamic_slice_in_dim(blocks, offset, slot_group, 0)
        inputs_now = lax.dynamic_slice_in_dim(index_in, offset, slot_group, 0)
        outputs_now = lax.dynamic_slice_in_dim(index_out, offset, slot_group, 0)
        live = (offset + jnp.arange(slot_group, dtype=jnp.int32) < live_count).astype(jnp.float32)
        gathered = jnp.take(sources, inputs_now, axis=0)
        if transposed:
            products = jnp.einsum(
                "bji,bjh->bih", tiles_now, gathered, preferred_element_type=jnp.float32
            )
        else:
            products = jnp.einsum(
                "bij,bjh->bih", tiles_now, gathered, preferred_element_type=jnp.float32
            )
        products = products * live[:, None, None]
        return totals.at[outputs_now].add(products)

    start_value = jnp.zeros((outputs, blocks.shape[1], sources.shape[2]), jnp.float32)
    return lax.fori_loop(0, groups, advance, start_value)


def gate_grad(masked, preact):
    sigmoid_v = jax.nn.sigmoid(preact)
    values = masked.astype(jnp.float32) * sigmoid_v * (1.0 + preact * (1.0 - sigmoid_v))
    return values.astype(jnp.bfloat16)


def shards(features, weight, edge_tiles, tile_row, tile_col, tile_count, labels, cotangent):
    node_dev = features.shape[0]
    tile_size = edge_tiles.shape[3]
    in_width = features.shape[1]
    rows_count = lax.axis_size("row")
    cols_count = lax.axis_size("col")
    row_tiles = node_dev * cols_count // tile_size
    col_tiles = node_dev * rows_count // tile_size
    blocks = edge_tiles.reshape(edge_tiles.shape[2], tile_size, tile_size)
    rows_here = tile_row.reshape(tile_row.shape[2])
    cols_here = tile_col.reshape(tile_col.shape[2])
    live_count = tile_count.reshape(())
    column_block = lax.all_gather(features, "row", axis=0, tiled=True)
    column_block = column_block.reshape(col_tiles, tile_size, in_width)
    partial_value = tile_products(
        blocks, cols_here, rows_here, live_count, column_block, row_tiles, False
    )
    partial_value = partial_value.reshape(row_tiles * tile_size, in_width)
    labelled = (labels >= 0).astype(jnp.float32)[:, None]
    masked = (cotangent.astype(jnp.float32) * labelled).astype(jnp.bfloat16)
    aggregate = lax.psum_scatter(
        partial_value.astype(jnp.bfloat16), "col", scatter_dimension=0, tiled=True
    )
    preact = jnp.dot(aggregate, weight, preferred_element_type=jnp.float32)
    activation = jax.nn.silu(preact).astype(jnp.bfloat16)
    grad_pre = gate_grad(masked, preact)
    grad_proj = lax.dot_general(
        grad_pre, weight, (((1,), (1,)), ((), ())), preferred_element_type=jnp.float32
    ).astype(jnp.bfloat16)
    row_block = lax.all_gather(grad_proj, "col", axis=0, tiled=True)
    row_block = row_block.reshape(row_tiles, tile_size, in_width)
    backward = tile_products(blocks, rows_here, cols_here, live_count, row_block, col_tiles, True)
    backward = backward.reshape(col_tiles * tile_size, in_width)
    grad_features = lax.psum_scatter(
        backward.astype(jnp.bfloat16), "row", scatter_dimension=0, tiled=True
    )
    weight_term = lax.dot_general(
        aggregate, grad_pre, (((0,), (0,)), ((), ())), preferred_element_type=jnp.float32
    )
    scale_factor = float(node_dev * rows_count * cols_count) ** (-0.5)
    grad_weight = lax.psum(weight_term, ("row", "col")) * scale_factor
    return (activation, grad_features, grad_weight)


def solution(mesh):
    return jax.shard_map(
        shards,
        mesh=mesh,
        in_specs=(
            P(("row", "col"), None),
            P(),
            P("row", "col", None, None, None),
            P("row", "col", None),
            P("row", "col", None),
            P("row", "col"),
            P(("row", "col")),
            P(("row", "col"), None),
        ),
        out_specs=(P(("row", "col"), None), P(("row", "col"), None), P()),
        check_vma=False,
    )
```

profile of v0, /device:TPU:1, one launch (start us, length us, event | category | flops | bytes accessed | tf_op | source)
XLA Modules:
  0.0 720.5 jit_solution(5384773387231898028)
XLA Ops:
  7.2 0.7 all-gather.2.cloned.1.call-update
  8.6 85.9 %all-gather.2.cloned.1.call-done = bf16[4096,128]{1,0:T(8,128)(2,1)} async-done(((bf16[128,128]{1,0:T(8,128)(2,1)}), bf16[4096,128]{1,0:T(8,128)(2,1)}) %all-gather.2.cloned.1.call-update) | async-done | bytes 1048592 | tf_op jit(solution)/shard_map/all_gather | solution.py:52
  94.6 42.7 %while.20 = (s32[]{:T(128)}, f32[16,128,128]{2,1,0:T(8,128)S(1)}, s32[]{:T(128)}, s32[144]{0:T(256)}, bf16[144,128,128]{2,1,0:T(8,128)(2,1)}, /*index=5*/s32[144...) while((s32[]{:T(128)}, f32[16,128,128]{2,1,0:T(8,128)S(1)}, ...), condition=%wide.region_2.3_spmd, body=%wide.region_0.2_spmd.sunk | while | flops 67896520 | bytes 6296351 | solution.py:31
  94.6 0.8 compare_select_fusion.8
  95.4 1.4 compare_and_fusion.4
  96.8 1.9 gather_fusion
  98.7 1.4 convolution_multiply_fusion.4
  100.1 1.6 scatter_fusion
  101.7 0.8 compare_select_fusion.8
  102.5 1.4 compare_and_fusion.4
  103.9 1.9 gather_fusion
  105.8 1.4 convolution_multiply_fusion.4
  107.2 1.6 scatter_fusion
  108.8 0.8 compare_select_fusion.8
  109.6 1.4 compare_and_fusion.4
  111.0 1.9 gather_fusion
  112.9 1.4 convolution_multiply_fusion.4
  114.3 1.6 scatter_fusion
  115.9 0.8 compare_select_fusion.8
  116.7 1.4 compare_and_fusion.4
  118.1 1.9 gather_fusion
  120.0 1.4 convolution_multiply_fusion.4
  121.4 1.6 scatter_fusion
  123.0 0.8 compare_select_fusion.8
  123.8 1.4 compare_and_fusion.4
  125.2 1.9 gather_fusion
  127.1 1.4 convolution_multiply_fusion.4
  128.5 1.6 scatter_fusion
  130.1 0.8 compare_select_fusion.8
  130.9 1.4 compare_and_fusion.4
  132.3 1.9 gather_fusion
  134.2 1.4 convolution_multiply_fusion.4
  135.6 1.6 scatter_fusion
  137.2 0.9 convert_element_type.47
  138.2 6.7 copy.11
  144.9 73.5 %reduce-scatter.3.cloned.1.call-done = bf16[128,128]{1,0:T(8,128)(2,1)} async-done(((bf16[2048,128]{1,0:T(8,128)(2,1)}), bf16[128,128]{1,0:T(8,128)(2,1)}) %reduce-scatter.3.cloned.1.call-update) | async-done | bytes 32784 | tf_op jit(solution)/shard_map/reduce_scatter | solution.py:60
  218.4 1.6 multiply_convert_fusion
  220.2 17.9 %all_gather.7 = bf16[2048,128]{1,0:T(8,128)(2,1)S(1)} all-gather(bf16[128,128]{1,0:T(8,128)(2,1)S(1)} %convolution_convert_fusion), channel_id=1, replica_groups=mesh['row'=32,'col'=16] {'col'}, dimensions={0}, use_global_device_ids=true | all-gather | bytes 557056 | tf_op jit(solution)/shard_map/all_gather | solution.py:69
  238.1 1.6 fusion.12
  239.8 1.6 broadcast_in_dim.40
  241.5 37.5 %while.21 = (s32[]{:T(128)}, f32[32,128,128]{2,1,0:T(8,128)}, s32[]{:T(128)}, s32[144]{0:T(256)S(1)}, bf16[144,128,128]{1,2,0:T(8,128)(2,1)}, /*index=5*/s32[144...) while((s32[]{:T(128)}, f32[32,128,128]{2,1,0:T(8,128)}, ...), condition=%wide.region_6.7_spmd, body=%wide.region_4.6_spmd.sunk | while | flops 67896520 | bytes 6296351 | solution.py:31
  241.5 0.7 compare_and_fusion.5
  242.9 1.4 convolution_multiply_fusion.5
  244.3 3.4 scatter_fusion.1
  247.8 0.7 compare_and_fusion.5
  249.2 1.4 convolution_multiply_fusion.5
  250.6 3.4 scatter_fusion.1
  254.0 0.7 compare_and_fusion.5
  254.8 0.6 gather_fusion.1
  255.4 1.4 convolution_multiply_fusion.5
  256.8 3.4 scatter_fusion.1
  260.3 0.7 compare_and_fusion.5
  261.7 1.4 convolution_multiply_fusion.5
  263.1 3.4 scatter_fusion.1
  266.5 0.7 compare_and_fusion.5
  267.9 1.4 convolution_multiply_fusion.5
  269.3 3.3 scatter_fusion.1
  272.8 0.7 compare_and_fusion.5
  274.1 1.4 convolution_multiply_fusion.5
  275.6 3.4 scatter_fusion.1
  279.0 2.7 convert_element_type.56
  281.7 218.8 %all-reduce.2.cloned.1.call-done = f32[128,256]{1,0:T(8,128)} async-done(((f32[128,256]{1,0:T(8,128)}), f32[128,256]{1,0:T(8,128)}) %all-reduce.2.cloned.1.call-update) | async-done | bytes 131088 | tf_op jit(solution)/shard_map/psum | solution.py:80
  500.5 1.6 broadcast_multiply_fusion
  502.1 211.9 %reduce-scatter.5.cloned.1.call-done = bf16[128,128]{1,0:T(8,128)(2,1)} async-done(((bf16[4096,128]{1,0:T(8,128)(2,1)}), bf16[128,128]{1,0:T(8,128)(2,1)}) %reduce-scatter.5.cloned.1.call-update) | async-done | bytes 32784 | tf_op jit(solution)/shard_map/reduce_scatter | solution.py:73
  (43 shorter events, 4.2 us)
Async XLA Ops:
  7.2 211.3 %copy-start = (bf16[128,256]{1,0:T(8,128)(2,1)S(1)}, bf16[128,256]{1,0:T(8,128)(2,1)}, u32[]{:S(2)}) copy-start(bf16[128,256]{1,0:T(8,128)(2,1)} %param.13) | copy-start | bytes 196612
  7.2 87.3 %all-gather.2.cloned.1.call-start = ((), (), s32[]{:S(2)}) async-start(), calls=%async_computation.2 | async-start | bytes 1081344 | tf_op jit(solution)/shard_map/all_gather | solution.py:52
  7.9 210.5 %reduce-scatter.3.cloned.1.call-start = ((), (), s32[]{:S(2)}) async-start(), calls=%async_computation.3 | async-start | bytes 557056 | tf_op jit(solution)/shard_map/reduce_scatter | solution.py:60
  138.2 362.4 %all-reduce.2.cloned.1.call-start = ((), (), s32[]{:S(2)}) async-start(), calls=%async_computation.5 | async-start | bytes 262144 | tf_op jit(solution)/shard_map/psum | solution.py:80
  138.2 6.7 copy-start.4
  138.2 80.2 %copy-start.3 = (bf16[128,256]{1,0:T(8,128)(2,1)S(1)}, bf16[128,256]{1,0:T(8,128)(2,1)}, u32[]{:S(2)}) copy-start(bf16[128,256]{1,0:T(8,128)(2,1)} %param.19) | copy-start | bytes 196612
  144.9 96.5 %copy-start.1 = (s32[144]{0:T(256)S(1)}, s32[144]{0:T(256)}, u32[]{:S(2)}) copy-start(s32[144]{0:T(256)} %get-tuple-element.339) | copy-start | bytes 1732
  144.9 96.5 %copy-start.2 = (s32[144]{0:T(256)S(1)}, s32[144]{0:T(256)}, u32[]{:S(2)}) copy-start(s32[144]{0:T(256)} %get-tuple-element.340) | copy-start | bytes 1732
  239.8 474.2 %reduce-scatter.5.cloned.1.call-start = ((), (), s32[]{:S(2)}) async-start(), calls=%async_computation.4 | async-start | bytes 1081344 | tf_op jit(solution)/shard_map/reduce_scatter | solution.py:73
Sparse Core Ops, SparseCore 0:
  11.2 83.2 all-gather.1
  138.3 80.0 reduce-scatter.2
  239.9 260.6 all-reduce.1
  505.4 208.5 reduce-scatter.4
where the time goes:
time: 728 us; the launch traced here: 721 us
  waiting for transfers between devices  591 us (81%)
  other arithmetic  52.8 us (7%)
  local copies, waits for them, and re-layouts  23.5 us (3%)
  matrix products  20.4 us (3%)
  blocking collectives  17.9 us (2%)
  between operations  14.5 us (2%)
    psum x1, waiting for transfers between devices, shards(): grad_weight = lax.psum(weight_term, ('row', 'col')) * scale_factor  219 us
    reduce_scatter x1, waiting for transfers between devices, shards(): lax.psum_scatter(backward.astype(jnp.bfloat16), 'row', scatter_dimension=...  212 us
    all_gather x1, waiting for transfers between devices, shards(): column_block = lax.all_gather(features, 'row', axis=0, tiled=True)  85.9 us
    reduce_scatter x1, waiting for transfers between devices, shards(): lax.psum_scatter(partial_value.astype(jnp.bfloat16), 'col', scatter_dimen...  73.5 us
    scatter-add x12, other arithmetic, advance(): return totals.at[outputs_now].add(products)  29.8 us
    all_gather x1, blocking collectives, shards(): row_block = lax.all_gather(grad_proj, 'col', axis=0, tiled=True)  17.9 us
    gather x12, local copies, waits for them, and re-layouts, advance(): gathered = jnp.take(sources, inputs_now, axis=0)  15.1 us
  transfers between devices with their start and end apart: 4, of which 4 were waited for; matrix products, arithmetic and copies ran while one was open for 7% of the time, Pallas kernels for 0%

commit v1 on v0

v1 whole, which is shorter than its diff:
```python
import jax
import jax.numpy as jnp
from jax import lax
from jax.experimental import pallas as pl
from jax.experimental.pallas import tpu as pltpu
from jax.sharding import PartitionSpec as P

MESH = pl.DeviceIdType.MESH
NX, NZ, NY = 4, 8, 8
T = 128
WIDE = 256
RING8 = (4, 3, 5, 2, 6, 1, 7)
RING4 = (2, 1, 3)
UNROLL = 8
BF, F32, I32 = jnp.bfloat16, jnp.float32, jnp.int32


def iota(shape, dim):
    return lax.broadcasted_iota(I32, shape, dim)


def mm(a, b):
    return jnp.dot(a, b, preferred_element_type=F32)


def mm_t(a, b):
    return lax.dot_general(a, b, (((1,), (1,)), ((), ())), preferred_element_type=F32)


def one_hot(mask):
    return jnp.where(mask, 1.0, 0.0).astype(BF)


def make_plan(keys, others, live, empty, out):
    groups = one_hot((iota((T, WIDE), 0) == keys) & live)
    before = one_hot(iota((WIDE, WIDE), 0) < iota((WIDE, WIDE), 1))
    rank = mm(groups, before)
    count = mm(groups, jnp.ones((WIDE, T), BF))
    padded = 2.0 * jnp.floor((count + 1.0) * 0.5)
    lower = one_hot(iota((T, T), 1) < iota((T, T), 0))
    start = mm(lower, padded.astype(BF))
    hot = groups.astype(F32)
    rank_here = jnp.sum(hot * rank, axis=0, keepdims=True)
    place = rank_here + jnp.sum(hot * start[:, :1], axis=0, keepdims=True)
    chosen = one_hot((iota((WIDE, WIDE), 0) == place.astype(I32)) & live)
    which = iota((8, WIDE), 0)
    slot = iota((8, WIDE), 1).astype(F32)
    rows = jnp.where(which == 0, slot, jnp.where(which == 1, others.astype(F32), jnp.where(
        which == 2, jnp.where(rank_here == 0.0, 1.0, 0.0), 1.0)))
    sorted_rows = mm_t(rows.astype(BF), chosen)
    count_row = mm_t(jnp.ones((8, WIDE), BF), groups)
    padded_row = 2.0 * jnp.floor((count_row + 1.0) * 0.5)
    upper = one_hot(iota((T, T), 0) < iota((T, T), 1))
    end_row = mm(padded_row.astype(BF), upper) + padded_row
    last_row = jnp.maximum(end_row * 0.5 - 1.0, 0.0)
    valid = sorted_rows[3:4] > 0.5
    out[0:1, :] = sorted_rows[0:1].astype(I32)
    out[1:2, :] = jnp.where(valid, sorted_rows[1:2], float(empty)).astype(I32)
    out[2:3, :] = (1.0 - sorted_rows[2:3]).astype(I32)
    out[3:4, 0:T] = last_row[0:1].astype(I32)
    out[4:5, 0:T] = jnp.where(count_row[0:1] > 0.5, 1.0, 0.0).astype(I32)


def kernel(features, weight, tiles, tile_row, tile_col, tile_count, labels, cotangent,
           act_out, gf_out, gw_out,
           tile_buf, xbuf, gbuf, pref, pblk, cr, ystage, yr, bblk, xr, zstage, zr, wbuf, cbuf, slots,
           plan_v, plan_f, plan_b, wt, w0r, wh, w1r, w2b, w3b, gw, act_v, gf_v,
           loc, ag_s, ag_r, c_s, c_r, y_s, y_r, g_s, g_r, x_s, x_r, z_s, z_r,
           w_s, w0_r, w1_r, w2_r, w3_r, w4_r, w5_r):
    r, c = lax.axis_index("row"), lax.axis_index("col")
    x, z, y, k = r // NZ, r % NZ, c // 2, c % 2
    other = 1 - k

    def at_x(d):
        return (((x + d) % NX) * NZ + z, c)

    def at_z(d):
        return (x * NZ + (z + d) % NZ, c)

    def at_y(d):
        return (r, ((y + d) % NY) * 2 + k)

    sibling = (r, y * 2 + other)
    sends = []

    def push(src, dst, ssem, rsem, device):
        copy = pltpu.make_async_remote_copy(src_ref=src, dst_ref=dst, send_sem=ssem, recv_sem=rsem,
                                            device_id=device, device_id_type=MESH)
        copy.start()
        sends.append(copy)

    def arrived(dst, sem):
        pltpu.make_async_remote_copy(src_ref=dst, dst_ref=dst, send_sem=sem, recv_sem=sem,
                                     device_id=sibling, device_id_type=MESH).wait_recv()

    barrier = pltpu.get_barrier_semaphore()
    partners = [at_z(d) for d in RING8] + [at_x(d) for d in RING4] + [at_y(d) for d in RING8] + [sibling]
    for device in partners:
        pl.semaphore_signal(barrier, inc=1, device_id=device, device_id_type=MESH)
    own = pltpu.make_async_copy(features, xbuf.at[0], loc.at[0])
    own.start()
    part = tiles.shape[0] // 4
    edge = [pltpu.make_async_copy(tiles.at[pl.ds(i * part, part)], tile_buf.at[pl.ds(i * part, part)], loc.at[1 + i])
            for i in range(4)]
    wcopy = pltpu.make_async_copy(weight, wbuf, loc.at[5])
    ccopy = pltpu.make_async_copy(cotangent, cbuf, loc.at[6])
    own.wait()
    pl.semaphore_wait(barrier, len(partners))

    for dz in RING8:
        push(xbuf.at[0], xbuf.at[dz], ag_s.at[dz], ag_r.at[dz], at_z(dz))
    for dx in RING4:
        push(xbuf.at[0], xbuf.at[dx * NZ], ag_s.at[dx * NZ], ag_r.at[dx * NZ], at_x(dx))
    for copy in edge + [wcopy, ccopy]:
        copy.start()

    slots[...] = jnp.zeros_like(slots)
    plan_v[...] = jnp.zeros_like(plan_v)
    slots[0:1, 0:tile_row.shape[1]] = tile_row[...]
    slots[1:2, 0:tile_row.shape[1]] = tile_col[...]
    rows_here, cols_here = slots[0:1, :], slots[1:2, :]
    live = iota((1, WIDE), 1) < tile_count[0, 0]
    xbuf[NX * NZ] = jnp.zeros((T, T), BF)
    gbuf[NY * 2] = jnp.zeros((T, T), BF)
    to_row = ((rows_here // 2 - y + NY) % NY) * 2 + (rows_here + k) % 2
    from_row = ((y - rows_here // 2 + NY) % NY) * 2 + (rows_here + k) % 2
    to_col = ((cols_here // NZ - x + NX) % NX) * NZ + (cols_here - z + NZ) % NZ
    from_col = ((x - cols_here // NZ + NX) % NX) * NZ + (z - cols_here + 4 * NZ) % NZ
    make_plan(to_row, from_col, live, NX * NZ, plan_v.at[0])
    make_plan(to_col, from_row, live, NY * 2, plan_v.at[1])
    fcopy = pltpu.make_async_copy(plan_v.at[0], plan_f, loc.at[7])
    bcopy = pltpu.make_async_copy(plan_v.at[1], plan_b, loc.at[8])
    fcopy.start()
    bcopy.start()

    for dz in (1, 7, 2, 6, 3, 5, 4):
        arrived(xbuf.at[dz], ag_r.at[dz])
        for dx in RING4:
            s = dx * NZ + dz
            push(xbuf.at[dz], xbuf.at[s], ag_s.at[s], ag_r.at[s], at_x(dx))
    for copy in edge + [wcopy, ccopy, fcopy, bcopy]:
        copy.wait()
    for dz in (0, 1, 7, 2, 6, 3, 5, 4):
        for dx in (1, 3, 2):
            arrived(xbuf.at[dx * NZ + dz], ag_r.at[dx * NZ + dz])

    def within(index, size):
        return jnp.minimum(jnp.maximum(index, 0), size - 1)

    def run(plan, pairs, blocks, product):
        def body(step, total):
            for u in range(UNROLL):
                pair = step * UNROLL + u
                first, second = 2 * pair, 2 * pair + 1
                value = product(
                    within(plan[0, first], tile_buf.shape[0]), within(plan[0, second], tile_buf.shape[0]),
                    within(plan[1, first], blocks), within(plan[1, second], blocks))
                total = jnp.where(plan[2, first] > 0, total, 0.0) + value
                pref[pair] = total
            return total

        lax.fori_loop(0, pairs // UNROLL, body, jnp.zeros((T, T), F32))

    def result(plan, group):
        return jnp.where(plan[4, group] > 0, pref[within(plan[3, group], pref.shape[0])], 0.0).astype(BF)

    def forward(s0, s1, b0, b1):
        return mm(jnp.concatenate([tile_buf[s0], tile_buf[s1]], axis=1),
                  jnp.concatenate([xbuf[b0], xbuf[b1]], axis=0))

    def backward(s0, s1, b0, b1):
        return mm(jnp.concatenate([gbuf[b0], gbuf[b1]], axis=1),
                  jnp.concatenate([tile_buf[s0], tile_buf[s1]], axis=0))

    slots_all = tiles.shape[0]
    run(plan_f, (slots_all + NY * 2) // 2, xbuf.shape[0], forward)

    for ey in RING8 + (0,):
        pblk[ey * 2 + 1] = result(plan_f, ey * 2 + 1)
        push(pblk.at[ey * 2 + 1], cr.at[ey], c_s.at[ey], c_r.at[ey], sibling)
    for ey in RING8 + (0,):
        pblk[ey * 2] = result(plan_f, ey * 2)
    for ey in RING8:
        arrived(cr.at[ey], c_r.at[ey])
        ystage[ey] = (pblk[ey * 2].astype(F32) + cr[ey].astype(F32)).astype(BF)
        push(ystage.at[ey], yr.at[ey], y_s.at[ey], y_r.at[ey], at_y(ey))
    arrived(cr.at[0], c_r.at[0])
    total = pblk[0].astype(F32) + cr[0].astype(F32)
    diagonal = jnp.where(iota((T, T), 0) == iota((T, T), 1), jnp.where(labels[...] >= 0, 1.0, 0.0), 0.0).astype(BF)
    masked = cbuf[...].astype(F32) * mm(diagonal, jnp.ones((T, WIDE), BF))
    for ey in (1, 7, 2, 6, 3, 5, 4):
        arrived(yr.at[ey], y_r.at[ey])
        total = total + yr[ey].astype(F32)
    aggregate = total.astype(BF)
    preact = mm(aggregate, wbuf[...])
    sigmoid_v = jax.nn.sigmoid(preact)
    grad_pre = (masked * sigmoid_v * (1.0 + preact * (1.0 - sigmoid_v))).astype(BF)
    gbuf[0] = mm_t(wbuf[...], grad_pre).astype(BF)

    for dy in RING8:
        push(gbuf.at[0], gbuf.at[dy * 2], g_s.at[dy * 2], g_r.at[dy * 2], at_y(dy))
    push(gbuf.at[0], gbuf.at[1], g_s.at[1], g_r.at[1], sibling)
    act_v[...] = (preact * sigmoid_v).astype(BF)
    acopy = pltpu.make_async_copy(act_v, act_out, loc.at[9])
    acopy.start()
    wt[...] = lax.dot_general(aggregate, grad_pre, (((0,), (0,)), ((), ())), preferred_element_type=F32)
    half = T // 2
    mine = pl.ds(pl.multiple_of(k * half, half), half)
    theirs = pl.ds(pl.multiple_of(other * half, half), half)
    push(wt.at[theirs], w0r, w_s.at[0], w0_r, sibling)
    arrived(w0r, w0_r)
    wh[...] = wt[mine, :] + w0r[...]
    piece = half // NY

    def rows_of(d):
        return pl.ds(pl.multiple_of(((y + d) % NY) * piece, piece), piece)

    for ey in RING8:
        push(wh.at[rows_of(ey)], w1r.at[ey], w_s.at[ey], w1_r.at[ey], at_y(ey))
    for dy in (1, 7, 2, 6, 3, 5, 4):
        arrived(gbuf.at[dy * 2], g_r.at[dy * 2])
        push(gbuf.at[dy * 2], gbuf.at[dy * 2 + 1], g_s.at[dy * 2 + 1], g_r.at[dy * 2 + 1], sibling)
    for dy in (0, 1, 7, 2, 6, 3, 5, 4):
        arrived(gbuf.at[dy * 2 + 1], g_r.at[dy * 2 + 1])
    term = wh[rows_of(0), :]
    for ey in RING8:
        arrived(w1r.at[ey], w1_r.at[ey])
        term = term + w1r[ey]
    w2b[z] = term
    for dz in RING8:
        push(w2b.at[z], w2b.at[z], w_s.at[8 + dz], w2_r.at[dz], at_z(dz))

    run(plan_b, (slots_all + NX * NZ) // 2, gbuf.shape[0], backward)

    for ez in RING8 + (0,):
        for ex in RING4:
            g = ex * NZ + ez
            bblk[g] = result(plan_b, g)
            push(bblk.at[g], xr.at[g], x_s.at[g], x_r.at[g], at_x(ex))
    for ez in range(NZ):
        bblk[ez] = result(plan_b, ez)
    for dz in RING8:
        arrived(w2b.at[(z + NZ - dz) % NZ], w2_r.at[dz])
    term = w2b[0]
    for i in range(1, NZ):
        term = term + w2b[i]
    w3b[x] = term
    for dx in RING4:
        push(w3b.at[x], w3b.at[x], w_s.at[16 + dx], w3_r.at[dx], at_x(dx))

    def x_total(ez):
        total = bblk[ez].astype(F32)
        for ex in (1, 3, 2):
            g = ex * NZ + ez
            arrived(xr.at[g], x_r.at[g])
            total = total + xr[g].astype(F32)
        return total

    for ez in RING8:
        zstage[ez] = x_total(ez).astype(BF)
        push(zstage.at[ez], zr.at[ez], z_s.at[ez], z_r.at[ez], at_z(ez))
    total = x_total(0)
    for dx in RING4:
        arrived(w3b.at[(x + NX - dx) % NX], w3_r.at[dx])
    term = w3b[0]
    for i in range(1, NX):
        term = term + w3b[i]

    def gw_rows(d):
        return pl.ds(pl.multiple_of(k * half + ((y + NY + d) % NY) * piece, piece), piece)

    gw[gw_rows(0), :] = term * (float(T * NX * NZ * NY * 2) ** -0.5)
    for dy in RING8:
        push(gw.at[gw_rows(0)], gw.at[gw_rows(0)], w_s.at[20 + dy], w4_r.at[dy], at_y(dy))
    for dy in RING8:
        arrived(gw.at[gw_rows(-dy)], w4_r.at[dy])
    push(gw.at[mine], gw.at[mine], w_s.at[28], w5_r, sibling)
    for ez in (1, 7, 2, 6, 3, 5, 4):
        arrived(zr.at[ez], z_r.at[ez])
        total = total + zr[ez].astype(F32)
    gf_v[...] = jnp.transpose(total).astype(BF)
    ocopy = pltpu.make_async_copy(gf_v, gf_out, loc.at[10])
    ocopy.start()
    arrived(gw.at[theirs], w5_r)
    gcopy = pltpu.make_async_copy(gw, gw_out, loc.at[11])
    gcopy.start()
    for copy in sends:
        copy.wait_send()
    acopy.wait()
    ocopy.wait()
    gcopy.wait()


def shards(features, weight, edge_tiles, tile_row, tile_col, tile_count, labels, cotangent):
    count = edge_tiles.shape[2]
    nodes, width = features.shape
    hidden = weight.shape[1]
    pairs = (count + NX * NZ) // 2
    dma = pltpu.SemaphoreType.DMA
    anywhere = pl.BlockSpec(memory_space=pl.ANY)
    vmem = pl.BlockSpec(memory_space=pltpu.VMEM)
    smem = pl.BlockSpec(memory_space=pltpu.SMEM)
    V = pltpu.VMEM
    return pl.pallas_call(
        kernel,
        out_shape=(
            jax.ShapeDtypeStruct((nodes, hidden), BF),
            jax.ShapeDtypeStruct((nodes, width), BF),
            jax.ShapeDtypeStruct((width, hidden), F32),
        ),
        in_specs=[anywhere, anywhere, anywhere, vmem, vmem, smem, vmem, anywhere],
        out_specs=(anywhere, anywhere, anywhere),
        scratch_shapes=[
            V((count, T, T), BF),
            V((NX * NZ + 1, T, T), BF),
            V((NY * 2 + 1, T, T), BF),
            V((pairs, T, T), F32),
            V((NY * 2, T, T), BF),
            V((NY, T, T), BF),
            V((NY, T, T), BF),
            V((NY, T, T), BF),
            V((NX * NZ, T, T), BF),
            V((NX * NZ, T, T), BF),
            V((NZ, T, T), BF),
            V((NZ, T, T), BF),
            V((width, hidden), BF),
            V((nodes, hidden), BF),
            V((8, WIDE), I32),
            V((2, 8, WIDE), I32),
            pltpu.SMEM((8, WIDE), I32),
            pltpu.SMEM((8, WIDE), I32),
            V((width, hidden), F32),
            V((width // 2, hidden), F32),
            V((width // 2, hidden), F32),
            V((NY, width // 2 // NY, hidden), F32),
            V((NZ, width // 2 // NY, hidden), F32),
            V((NX, width // 2 // NY, hidden), F32),
            V((width, hidden), F32),
            V((nodes, hidden), BF),
            V((nodes, width), BF),
            dma((12,)),
            dma((NX * NZ,)), dma((NX * NZ,)),
            dma((NY,)), dma((NY,)),
            dma((NY,)), dma((NY,)),
            dma((NY * 2,)), dma((NY * 2,)),
            dma((NX * NZ,)), dma((NX * NZ,)),
            dma((NZ,)), dma((NZ,)),
            dma((30,)),
            dma, dma((NY,)), dma((NZ,)), dma((NX,)), dma((NY,)), dma,
        ],
        compiler_params=pltpu.CompilerParams(
            collective_id=0, has_side_effects=True, vmem_limit_bytes=48 * 1024 * 1024
        ),
    )(features, weight, edge_tiles.reshape(count, T, T), tile_row.reshape(1, count), tile_col.reshape(1, count),
      tile_count, labels.reshape(1, nodes), cotangent)


def solution(mesh):
    return jax.shard_map(
        shards,
        mesh=mesh,
        in_specs=(
            P(("row", "col"), None),
            P(),
            P("row", "col", None, None, None),
            P("row", "col", None),
            P("row", "col", None),
            P("row", "col"),
            P(("row", "col")),
            P(("row", "col"), None),
        ),
        out_specs=(P(("row", "col"), None), P(("row", "col"), None), P()),
        check_vma=False,
    )
```

time: 728 us -> 93.6 us (0.13)
  waiting for transfers between devices: 591 us -> 0 us
  Pallas kernels: 0 us -> 83.2 us
  other arithmetic: 52.8 us -> 0 us
  matrix products: 20.4 us -> 0 us
  blocking collectives: 17.9 us -> 0 us
  local copies, waits for them, and re-layouts: 23.5 us -> 8.68 us
  between operations: 14.5 us -> 1.3 us
    reduce_scatter x2 -> x0, waiting for transfers between devices: 285 us -> none  [the longest x1 212 us: shards(): lax.psum_scatter(backward.astype(jnp.bfloat16), 'row', scatter_dimension=...]
    psum x1 -> x0, waiting for transfers between devices: 219 us -> none  [shards(): grad_weight = lax.psum(weight_term, ('row', 'col')) * scale_factor]
    all_gather x1 -> x0, waiting for transfers between devices: 85.9 us -> none  [shards(): column_block = lax.all_gather(features, 'row', axis=0, tiled=True)]
    pallas_call x0 -> x1, Pallas kernels: none -> 83.2 us  [shards(): pl.pallas_call(kernel, out_shape=(jax.ShapeDtypeStruct((nodes, hidden), B...]
    scatter-add x12 -> x0, other arithmetic: 29.8 us -> none  [advance(): return totals.at[outputs_now].add(products)]
    dot_general x15 -> x0, matrix products: 20.4 us -> none  [the longest x6 8.51 us: advance(): jnp.einsum('bji,bjh->bih', tiles_now, gathered, preferred_element_type=jn...]
    all_gather x1 -> x0, blocking collectives: 17.9 us -> none  [shards(): row_block = lax.all_gather(grad_proj, 'col', axis=0, tiled=True)]
    gather x12 -> x0, local copies, waits for them, and re-layouts: 15.1 us -> none  [advance(): gathered = jnp.take(sources, inputs_now, axis=0)]
  transfers between devices with their start and end apart: 4 -> 0, of which waited for: 4 -> 0; matrix products, arithmetic and copies ran while one was open for 7% -> 0% of each run, Pallas kernels for 0% -> 0%
where the time goes in v1:
time: 93.6 us; the launch traced here: 93.2 us
  Pallas kernels  83.2 us (89%)
  local copies, waits for them, and re-layouts  8.68 us (9%)
  between operations  1.3 us (1%)
    pallas_call x1, Pallas kernels, shards(): pl.pallas_call(kernel, out_shape=(jax.ShapeDtypeStruct((nodes, hidden), B...  83.2 us
    unnamed x17, local copies, waits for them, and re-layouts  8.68 us

profile of v1, /device:TPU:1, one launch (start us, length us, event | category | flops | bytes accessed | tf_op | source)
XLA Modules:
  0.0 93.2 jit_solution(13857322856811020251)
XLA Ops:
  1.3 0.0 copy-start
  1.3 2.3 %copy-done = bf16[1,1,144,128,128]{4,3,2,1,0:T(8,128)(2,1)S(1)} copy-done((bf16[1,1,144,128,128]{4,3,2,1,0:T(8,128)(2,1)S(1)}, bf16[1,1,144,128,128]{4,3,2,1,0:T(8,128)(2,1)}, u32[]{:S(2)}) %copy-start) | copy-done | bytes 4718616
  3.6 0.0 copy-start.1
  3.6 0.8 copy-done.1
  4.5 0.0 copy-start.2
  4.5 0.8 copy-done.2
  5.3 0.0 copy-start.3
  5.3 0.8 copy-done.3
  6.1 0.0 copy-start.4
  6.1 0.7 copy-done.4
  6.7 0.0 copy-start.5
  6.7 0.7 copy-done.5
  7.4 0.0 copy-start.6
  7.4 0.7 copy-done.6
  8.1 83.2 %shard_map.103 = (bf16[128,256]{1,0:T(8,128)(2,1)S(1)}, bf16[128,128]{1,0:T(8,128)(2,1)S(1)}, f32[128,256]{1,0:T(8,128)S(1)}) custom-call(bf16[128,128]{1,0:T(8,128)(2,1)S(1)} %copy-done.3, bf16[128,256]{1,0:T(8,128)(2,1)S(1)} %copy-done.1, bf16[144,128,128]{2,1,0:T(8,128)(2,1)S(1)} %bitcast.4, s32[1,144]{1,0:T(1,128)S(1)} %bitcast.5, s32[1,144]{1,0:T(1,128)S(1)} %bitcast.6, ...), custom_call_target="tpu_custom_call" | custom-call | tf_op jit(solution)/shard_map/pallas_call | solution.py:304
  91.3 0.6 copy.15
  91.9 0.6 copy.16
  92.6 0.7 copy.17
Async XLA Ops:
  1.3 2.3 %copy-start = (bf16[1,1,144,128,128]{4,3,2,1,0:T(8,128)(2,1)S(1)}, bf16[1,1,144,128,128]{4,3,2,1,0:T(8,128)(2,1)}, u32[]{:S(2)}) copy-start(bf16[1,1,144,128,128]{4,3,2,1,0:T(8,128)(2,1)} %param.10) | copy-start | bytes 14155780
  3.6 0.8 copy-start.1
  4.5 0.8 copy-start.2
  5.3 0.8 copy-start.3
  6.1 0.7 copy-start.4
  6.7 0.7 copy-start.5
  7.4 0.7 copy-start.6

commit v2 on v1

v2 whole, which is shorter than its diff:
```python
import jax
import jax.numpy as jnp
from jax import lax
from jax.experimental import pallas as pl
from jax.experimental.pallas import tpu as pltpu
from jax.sharding import PartitionSpec as P

MESH = pl.DeviceIdType.MESH
NX, NZ, NY = 4, 8, 8
T = 128
WIDE = 256
RING8 = (4, 3, 5, 2, 6, 1, 7)
RING4 = (2, 1, 3)
FORWARD_STEP, BACKWARD_STEP = 20, 22
HALF = 64
BF, F32, I32 = jnp.bfloat16, jnp.float32, jnp.int32


def iota(shape, dim):
    return lax.broadcasted_iota(I32, shape, dim)


def mm(a, b):
    return jnp.dot(a, b, preferred_element_type=F32)


def mm_t(a, b):
    return lax.dot_general(a, b, (((1,), (1,)), ((), ())), preferred_element_type=F32)


def one_hot(mask):
    return jnp.where(mask, 1.0, 0.0).astype(BF)


def make_plan(keys, others, live, empty, out):
    groups = one_hot((iota((T, WIDE), 0) == keys) & live)
    before = one_hot(iota((WIDE, WIDE), 0) < iota((WIDE, WIDE), 1))
    rank = mm(groups, before)
    count = mm(groups, jnp.ones((WIDE, T), BF))
    padded = 2.0 * jnp.floor((count + 1.0) * 0.5)
    lower = one_hot(iota((T, T), 1) < iota((T, T), 0))
    start = mm(lower, padded.astype(BF))
    hot = groups.astype(F32)
    rank_here = jnp.sum(hot * rank, axis=0, keepdims=True)
    place = rank_here + jnp.sum(hot * start[:, :1], axis=0, keepdims=True)
    chosen = one_hot((iota((WIDE, WIDE), 0) == place.astype(I32)) & live)
    which = iota((8, WIDE), 0)
    slot = iota((8, WIDE), 1).astype(F32)
    rows = jnp.where(which == 0, slot, jnp.where(which == 1, others.astype(F32), jnp.where(
        which == 2, jnp.where(rank_here == 0.0, 1.0, 0.0), 1.0)))
    sorted_rows = mm_t(rows.astype(BF), chosen)
    count_row = mm_t(jnp.ones((8, WIDE), BF), groups)
    padded_row = 2.0 * jnp.floor((count_row + 1.0) * 0.5)
    upper = one_hot(iota((T, T), 0) < iota((T, T), 1))
    end_row = mm(padded_row.astype(BF), upper) + padded_row
    last_row = jnp.maximum(end_row * 0.5 - 1.0, 0.0)
    valid = sorted_rows[3:4] > 0.5
    out[0:1, :] = sorted_rows[0:1].astype(I32)
    out[1:2, :] = jnp.where(valid, sorted_rows[1:2], float(empty)).astype(I32)
    out[2:3, :] = (1.0 - sorted_rows[2:3]).astype(I32)
    out[3:4, 0:T] = last_row[0:1].astype(I32)
    out[4:5, 0:T] = jnp.where(count_row[0:1] > 0.5, 1.0, 0.0).astype(I32)


def kernel(features, weight, tiles, tile_row, tile_col, labels, cotangent, tile_count,
           act_out, gf_out, gw_out,
           tile_buf, xbuf, gbuf_a, gbuf_b, pref, pref2, pblk, cr, ystage, yr, bblk, xr, zstage, zr, wbuf, cbuf, slots,
           plan_v, plan_f, plan_b, wt, w0r, wh, w1r, w2b, w3b, rows_v, cols_v, labels_v,
           loc, ag_s, ag_r, c_s, c_r, y_s, y_r, g_s, g_r, x_s, x_r, z_s, z_r,
           w_s, w0_r, w1_r, w2_r, w3_r, w4_r, w5_r):
    r, c = lax.axis_index("row"), lax.axis_index("col")
    gbuf = (gbuf_a, gbuf_b)
    x, z, y, k = r // NZ, r % NZ, c // 2, c % 2
    other = 1 - k

    def at_x(d):
        return (((x + d) % NX) * NZ + z, c)

    def at_z(d):
        return (x * NZ + (z + d) % NZ, c)

    def at_y(d):
        return (r, ((y + d) % NY) * 2 + k)

    sibling = (r, y * 2 + other)
    sends = []

    def push(src, dst, ssem, rsem, device):
        copy = pltpu.make_async_remote_copy(src_ref=src, dst_ref=dst, send_sem=ssem, recv_sem=rsem,
                                            device_id=device, device_id_type=MESH)
        copy.start()
        sends.append(copy)

    def arrived(dst, sem):
        pltpu.make_async_remote_copy(src_ref=dst, dst_ref=dst, send_sem=sem, recv_sem=sem,
                                     device_id=sibling, device_id_type=MESH).wait_recv()

    own = pltpu.make_async_copy(features, xbuf.at[0], loc.at[0])
    own.start()
    barrier = pltpu.get_barrier_semaphore()
    partners = [at_z(d) for d in RING8] + [at_x(d) for d in RING4] + [at_y(d) for d in RING8] + [sibling]
    for device in partners:
        pl.semaphore_signal(barrier, inc=1, device_id=device, device_id_type=MESH)
    part = tiles.shape[0] // 4
    edge = [pltpu.make_async_copy(tiles.at[pl.ds(i * part, part)], tile_buf.at[pl.ds(i * part, part)], loc.at[1 + i])
            for i in range(4)]
    wcopy = pltpu.make_async_copy(weight, wbuf, loc.at[5])
    ccopy = pltpu.make_async_copy(cotangent, cbuf, loc.at[6])
    small = [pltpu.make_async_copy(a, b, loc.at[9 + i]) for i, (a, b) in enumerate(
        ((tile_row, rows_v), (tile_col, cols_v), (labels, labels_v)))]
    for copy in small + edge + [wcopy, ccopy]:
        copy.start()
    own.wait()
    pl.semaphore_wait(barrier, len(partners))

    for dz in RING8:
        push(xbuf.at[0], xbuf.at[dz], ag_s.at[dz], ag_r.at[dz], at_z(dz))
    for dx in RING4:
        push(xbuf.at[0], xbuf.at[dx * NZ], ag_s.at[dx * NZ], ag_r.at[dx * NZ], at_x(dx))
    for copy in small:
        copy.wait()
    slots[...] = jnp.zeros_like(slots)
    plan_v[...] = jnp.zeros_like(plan_v)
    slots[0:1, 0:tile_row.shape[1]] = rows_v[...]
    slots[1:2, 0:tile_row.shape[1]] = cols_v[...]
    rows_here, cols_here = slots[0:1, :], slots[1:2, :]
    live = iota((1, WIDE), 1) < tile_count[0, 0]
    xbuf[NX * NZ] = jnp.zeros((T, T), BF)
    for h in range(2):
        gbuf[h][NY * 2] = jnp.zeros((HALF, T), BF)
    to_row = ((rows_here // 2 - y + NY) % NY) * 2 + (rows_here + k) % 2
    from_row = ((y - rows_here // 2 + NY) % NY) * 2 + (rows_here + k) % 2
    to_col = ((cols_here // NZ - x + NX) % NX) * NZ + (cols_here - z + NZ) % NZ
    from_col = ((x - cols_here // NZ + NX) % NX) * NZ + (z - cols_here + 4 * NZ) % NZ
    make_plan(to_row, from_col, live, NX * NZ, plan_v.at[0])
    make_plan(to_col, from_row, live, NY * 2, plan_v.at[1])
    fcopy = pltpu.make_async_copy(plan_v.at[0], plan_f, loc.at[7])
    bcopy = pltpu.make_async_copy(plan_v.at[1], plan_b, loc.at[8])
    fcopy.start()
    bcopy.start()

    for dz in (1, 7, 2, 6, 3, 5, 4):
        arrived(xbuf.at[dz], ag_r.at[dz])
        for dx in RING4:
            s = dx * NZ + dz
            push(xbuf.at[dz], xbuf.at[s], ag_s.at[s], ag_r.at[s], at_x(dx))
    for copy in edge + [wcopy, ccopy, fcopy, bcopy]:
        copy.wait()
    for dz in (0, 1, 7, 2, 6, 3, 5, 4):
        for dx in (1, 3, 2):
            arrived(xbuf.at[dx * NZ + dz], ag_r.at[dx * NZ + dz])

    def within(index, size):
        return jnp.minimum(jnp.maximum(index, 0), size - 1)

    def run(plan, pairs, unroll, blocks, sums, product):
        def body(step, total):
            for u in range(unroll):
                pair = step * unroll + u
                first, second = 2 * pair, 2 * pair + 1
                value = product(
                    within(plan[0, first], tile_buf.shape[0]), within(plan[0, second], tile_buf.shape[0]),
                    within(plan[1, first], blocks), within(plan[1, second], blocks))
                total = jnp.where(plan[2, first] > 0, total, 0.0) + value
                sums[pair] = total
            return total

        lax.fori_loop(0, pairs // unroll, body, jnp.zeros(sums.shape[1:], F32))

    def result(plan, group, sums):
        return jnp.where(plan[4, group] > 0, sums[within(plan[3, group], sums.shape[0])], 0.0).astype(BF)

    def forward(s0, s1, b0, b1):
        return mm(jnp.concatenate([tile_buf[s0], tile_buf[s1]], axis=1),
                  jnp.concatenate([xbuf[b0], xbuf[b1]], axis=0))

    def backward(h):
        def product(s0, s1, b0, b1):
            return mm(jnp.concatenate([gbuf[h][b0], gbuf[h][b1]], axis=1),
                      jnp.concatenate([tile_buf[s0], tile_buf[s1]], axis=0))
        return product

    slots_all = tiles.shape[0]
    run(plan_f, (slots_all + NY * 2) // 2, FORWARD_STEP, xbuf.shape[0], pref, forward)

    for ey in RING8 + (0,):
        pblk[ey * 2 + 1] = result(plan_f, ey * 2 + 1, pref)
        push(pblk.at[ey * 2 + 1], cr.at[ey], c_s.at[ey], c_r.at[ey], sibling)
    for ey in RING8 + (0,):
        pblk[ey * 2] = result(plan_f, ey * 2, pref)
    for ey in RING8:
        arrived(cr.at[ey], c_r.at[ey])
        ystage[ey] = (pblk[ey * 2].astype(F32) + cr[ey].astype(F32)).astype(BF)
        push(ystage.at[ey], yr.at[ey], y_s.at[ey], y_r.at[ey], at_y(ey))
    arrived(cr.at[0], c_r.at[0])
    total = pblk[0].astype(F32) + cr[0].astype(F32)
    diagonal = jnp.where(iota((T, T), 0) == iota((T, T), 1), jnp.where(labels_v[...] >= 0, 1.0, 0.0), 0.0).astype(BF)
    masked = cbuf[...].astype(F32) * mm(diagonal, jnp.ones((T, WIDE), BF))
    for ey in (1, 7, 2, 6, 3, 5, 4):
        arrived(yr.at[ey], y_r.at[ey])
        total = total + yr[ey].astype(F32)
    aggregate = total.astype(BF)
    preact = mm(aggregate, wbuf[...])
    sigmoid_v = jax.nn.sigmoid(preact)
    grad_pre = (masked * sigmoid_v * (1.0 + preact * (1.0 - sigmoid_v))).astype(BF)
    projected = mm_t(wbuf[...], grad_pre).astype(BF)
    gbuf[0][0] = projected[:HALF]
    gbuf[1][0] = projected[HALF:]

    for h in range(2):
        for dy in RING8:
            push(gbuf[h].at[0], gbuf[h].at[dy * 2], g_s.at[h, dy * 2], g_r.at[h, dy * 2], at_y(dy))
        push(gbuf[h].at[0], gbuf[h].at[1], g_s.at[h, 1], g_r.at[h, 1], sibling)
    act_out[...] = (preact * sigmoid_v).astype(BF)
    wt[...] = lax.dot_general(aggregate, grad_pre, (((0,), (0,)), ((), ())), preferred_element_type=F32)
    half = T // 2
    mine = pl.ds(pl.multiple_of(k * half, half), half)
    theirs = pl.ds(pl.multiple_of(other * half, half), half)
    push(wt.at[theirs], w0r, w_s.at[0], w0_r, sibling)
    arrived(w0r, w0_r)
    wh[...] = wt[mine, :] + w0r[...]
    piece = half // NY

    def rows_of(d):
        return pl.ds(pl.multiple_of(((y + d) % NY) * piece, piece), piece)

    for ey in RING8:
        push(wh.at[rows_of(ey)], w1r.at[ey], w_s.at[ey], w1_r.at[ey], at_y(ey))
    def hand_on(h):
        for dy in (1, 7, 2, 6, 3, 5, 4):
            arrived(gbuf[h].at[dy * 2], g_r.at[h, dy * 2])
            push(gbuf[h].at[dy * 2], gbuf[h].at[dy * 2 + 1], g_s.at[h, dy * 2 + 1], g_r.at[h, dy * 2 + 1], sibling)

    def transposed_sums(h):
        for dy in (0, 1, 7, 2, 6, 3, 5, 4):
            arrived(gbuf[h].at[dy * 2 + 1], g_r.at[h, dy * 2 + 1])
        run(plan_b, (slots_all + NX * NZ) // 2, BACKWARD_STEP, gbuf[h].shape[0], pref2.at[h], backward(h))

    def send_x(h):
        for ez in RING8 + (0,):
            for ex in RING4:
                g = ex * NZ + ez
                bblk[h, g] = result(plan_b, g, pref2.at[h])
                push(bblk.at[h, g], xr.at[h, g], x_s.at[h, g], x_r.at[h, g], at_x(ex))
        for ez in range(NZ):
            bblk[h, ez] = result(plan_b, ez, pref2.at[h])

    hand_on(0)
    transposed_sums(0)
    hand_on(1)
    term = wh[rows_of(0), :]
    for ey in RING8:
        arrived(w1r.at[ey], w1_r.at[ey])
        term = term + w1r[ey]
    w2b[x] = term
    for dx in RING4:
        push(w2b.at[x], w2b.at[x], w_s.at[8 + dx], w2_r.at[dx], at_x(dx))

    send_x(0)
    transposed_sums(1)
    send_x(1)
    for dx in RING4:
        arrived(w2b.at[(x + NX - dx) % NX], w2_r.at[dx])
    term = w2b[0]
    for i in range(1, NX):
        term = term + w2b[i]
    w3b[z] = term
    for dz in RING8:
        push(w3b.at[z], w3b.at[z], w_s.at[12 + dz], w3_r.at[dz], at_z(dz))

    def x_total(h, ez):
        total = bblk[h, ez].astype(F32)
        for ex in (1, 3, 2):
            g = ex * NZ + ez
            arrived(xr.at[h, g], x_r.at[h, g])
            total = total + xr[h, g].astype(F32)
        return total

    def gw_rows(d):
        return pl.ds(pl.multiple_of(k * half + ((y + NY + d) % NY) * piece, piece), piece)

    def send_z(h):
        for ez in RING8:
            zstage[h, ez] = x_total(h, ez).astype(BF)
            push(zstage.at[h, ez], zr.at[h, ez], z_s.at[h, ez], z_r.at[h, ez], at_z(ez))

    send_z(0)
    for dz in RING8:
        arrived(w3b.at[(z + NZ - dz) % NZ], w3_r.at[dz])
    term = w3b[0]
    for i in range(1, NZ):
        term = term + w3b[i]
    gw_out[gw_rows(0), :] = term * (float(T * NX * NZ * NY * 2) ** -0.5)
    for dy in RING8:
        push(gw_out.at[gw_rows(0)], gw_out.at[gw_rows(0)], w_s.at[20 + dy], w4_r.at[dy], at_y(dy))
    total_a = x_total(0, 0)
    send_z(1)
    total_b = x_total(1, 0)
    for dy in RING8:
        arrived(gw_out.at[gw_rows(-dy)], w4_r.at[dy])
    push(gw_out.at[mine], gw_out.at[mine], w_s.at[28], w5_r, sibling)
    for ez in (1, 7, 2, 6, 3, 5, 4):
        arrived(zr.at[0, ez], z_r.at[0, ez])
        total_a = total_a + zr[0, ez].astype(F32)
    for ez in (1, 7, 2, 6, 3, 5, 4):
        arrived(zr.at[1, ez], z_r.at[1, ez])
        total_b = total_b + zr[1, ez].astype(F32)
    gf_out[...] = jnp.transpose(jnp.concatenate([total_a, total_b], axis=0)).astype(BF)
    arrived(gw_out.at[theirs], w5_r)
    for copy in sends:
        copy.wait_send()


def shards(features, weight, edge_tiles, tile_row, tile_col, tile_count, labels, cotangent):
    count = edge_tiles.shape[2]
    nodes, width = features.shape
    hidden = weight.shape[1]
    pairs = (count + NX * NZ) // 2
    dma = pltpu.SemaphoreType.DMA
    hbm = pl.BlockSpec(memory_space=pltpu.HBM)
    vmem = pl.BlockSpec(memory_space=pltpu.VMEM)
    V = pltpu.VMEM
    return pl.pallas_call(
        kernel,
        out_shape=(
            jax.ShapeDtypeStruct((nodes, hidden), BF),
            jax.ShapeDtypeStruct((nodes, width), BF),
            jax.ShapeDtypeStruct((width, hidden), F32),
        ),
        in_specs=[hbm] * 7 + [pl.BlockSpec(memory_space=pltpu.SMEM)],
        out_specs=(vmem, vmem, vmem),
        scratch_shapes=[
            V((count, T, T), BF),
            V((NX * NZ + 1, T, T), BF),
            V((NY * 2 + 1, HALF, T), BF),
            V((NY * 2 + 1, HALF, T), BF),
            V(((count + NY * 2) // 2, T, T), F32),
            V((2, pairs, HALF, T), F32),
            V((NY * 2, T, T), BF),
            V((NY, T, T), BF),
            V((NY, T, T), BF),
            V((NY, T, T), BF),
            V((2, NX * NZ, HALF, T), BF),
            V((2, NX * NZ, HALF, T), BF),
            V((2, NZ, HALF, T), BF),
            V((2, NZ, HALF, T), BF),
            V((width, hidden), BF),
            V((nodes, hidden), BF),
            V((8, WIDE), I32),
            V((2, 8, WIDE), I32),
            pltpu.SMEM((8, WIDE), I32),
            pltpu.SMEM((8, WIDE), I32),
            V((width, hidden), F32),
            V((width // 2, hidden), F32),
            V((width // 2, hidden), F32),
            V((NY, width // 2 // NY, hidden), F32),
            V((NX, width // 2 // NY, hidden), F32),
            V((NZ, width // 2 // NY, hidden), F32),
            V((1, count), I32), V((1, count), I32), V((1, nodes), I32),
            dma((13,)),
            dma((NX * NZ,)), dma((NX * NZ,)),
            dma((NY,)), dma((NY,)),
            dma((NY,)), dma((NY,)),
            dma((2, NY * 2)), dma((2, NY * 2)),
            dma((2, NX * NZ)), dma((2, NX * NZ)),
            dma((2, NZ)), dma((2, NZ)),
            dma((30,)),
            dma, dma((NY,)), dma((NX,)), dma((NZ,)), dma((NY,)), dma,
        ],
        compiler_params=pltpu.CompilerParams(
            collective_id=0, has_side_effects=True, vmem_limit_bytes=40 * 1024 * 1024
        ),
    )(*(pltpu.with_memory_space_constraint(a, pltpu.HBM) for a in (
        features, weight, edge_tiles.reshape(count, T, T), tile_row.reshape(1, count), tile_col.reshape(1, count),
        labels.reshape(1, nodes), cotangent)), tile_count)


def solution(mesh):
    return jax.shard_map(
        shards,
        mesh=mesh,
        in_specs=(
            P(("row", "col"), None),
            P(),
            P("row", "col", None, None, None),
            P("row", "col", None),
            P("row", "col", None),
            P("row", "col"),
            P(("row", "col")),
            P(("row", "col"), None),
        ),
        out_specs=(P(("row", "col"), None), P(("row", "col"), None), P()),
        check_vma=False,
    )
```

time: 93.6 us -> 78.9 us (0.84)
  Pallas kernels: 83.2 us -> 75.6 us
  local copies, waits for them, and re-layouts: 8.68 us -> 1.9 us
    pallas_call x1, Pallas kernels: 83.2 us -> 75.6 us  [shards(): pl.pallas_call(kernel, out_shape=(jax.ShapeDtypeStruct((nodes, hidden), B...]
    unnamed x17 -> x3, local copies, waits for them, and re-layouts: 8.68 us -> 1.9 us
where the time goes in v2:
time: 78.9 us; the launch traced here: 78.7 us
  Pallas kernels  75.6 us (96%)
  local copies, waits for them, and re-layouts  1.9 us (2%)
  between operations  1.29 us (2%)
    pallas_call x1, Pallas kernels, shards(): pl.pallas_call(kernel, out_shape=(jax.ShapeDtypeStruct((nodes, hidden), B...  75.6 us
    unnamed x3, local copies, waits for them, and re-layouts  1.9 us

profile of v2, /device:TPU:1, one launch (start us, length us, event | category | flops | bytes accessed | tf_op | source)
XLA Modules:
  0.0 78.7 jit_solution(2979290612393685827)
XLA Ops:
  1.3 75.6 %shard_map.103 = (bf16[128,256]{1,0:T(8,128)(2,1)S(1)}, bf16[128,128]{1,0:T(8,128)(2,1)S(1)}, f32[128,256]{1,0:T(8,128)S(1)}) custom-call(bf16[128,128]{1,0:T(8,128)(2,1)} %features.1, bf16[128,256]{1,0:T(8,128)(2,1)} %weight.1, bf16[144,128,128]{2,1,0:T(8,128)(2,1)} %bitcast.4, s32[1,144]{1,0:T(1,128)} %bitcast.5, s32[1,144]{1,0:T(1,128)} %bitcast.6, ...), custom_call_target="tpu_custom_call" | custom-call | tf_op jit(solution)/shard_map/pallas_call | solution.py:323
  76.8 0.6 copy.15
  77.5 0.6 copy.16
  78.1 0.7 copy.17

commit v3 on v2

--- a/solution.py
+++ b/solution.py
@@ -113,10 +113,15 @@
     own.wait()
     pl.semaphore_wait(barrier, len(partners))
 
-    for dz in RING8:
+    for dz in (1, 7, 2, 6, 3, 5, 4):
         push(xbuf.at[0], xbuf.at[dz], ag_s.at[dz], ag_r.at[dz], at_z(dz))
     for dx in RING4:
         push(xbuf.at[0], xbuf.at[dx * NZ], ag_s.at[dx * NZ], ag_r.at[dx * NZ], at_x(dx))
+    for dz in (1, 7, 2, 6, 3, 5, 4):
+        arrived(xbuf.at[dz], ag_r.at[dz])
+        for dx in RING4:
+            s = dx * NZ + dz
+            push(xbuf.at[dz], xbuf.at[s], ag_s.at[s], ag_r.at[s], at_x(dx))
     for copy in small:
         copy.wait()
     slots[...] = jnp.zeros_like(slots)
@@ -139,11 +144,6 @@
     fcopy.start()
     bcopy.start()
 
-    for dz in (1, 7, 2, 6, 3, 5, 4):
-        arrived(xbuf.at[dz], ag_r.at[dz])
-        for dx in RING4:
-            s = dx * NZ + dz
-            push(xbuf.at[dz], xbuf.at[s], ag_s.at[s], ag_r.at[s], at_x(dx))
     for copy in edge + [wcopy, ccopy, fcopy, bcopy]:
         copy.wait()
     for dz in (0, 1, 7, 2, 6, 3, 5, 4):
@@ -208,7 +208,7 @@
     gbuf[1][0] = projected[HALF:]
 
     for h in range(2):
-        for dy in RING8:
+        for dy in (1, 7, 2, 6, 3, 5, 4):
             push(gbuf[h].at[0], gbuf[h].at[dy * 2], g_s.at[h, dy * 2], g_r.at[h, dy * 2], at_y(dy))
         push(gbuf[h].at[0], gbuf[h].at[1], g_s.at[h, 1], g_r.at[h, 1], sibling)
     act_out[...] = (preact * sigmoid_v).astype(BF)

time: 78.9 us -> 73.3 us (0.929)
  Pallas kernels: 75.6 us -> 69.9 us
    pallas_call x1, Pallas kernels: 75.6 us -> 69.9 us  [shards(): pl.pallas_call(kernel, out_shape=(jax.ShapeDtypeStruct((nodes, hidden), B...]
where the time goes in v3:
time: 73.3 us; the launch traced here: 73.1 us
  Pallas kernels  69.9 us (95%)
  local copies, waits for them, and re-layouts  1.9 us (3%)
  between operations  1.29 us (2%)
    pallas_call x1, Pallas kernels, shards(): pl.pallas_call(kernel, out_shape=(jax.ShapeDtypeStruct((nodes, hidden), B...  69.9 us
    unnamed x3, local copies, waits for them, and re-layouts  1.9 us

profile of v3, /device:TPU:1, one launch (start us, length us, event | category | flops | bytes accessed | tf_op | source)
XLA Modules:
  0.0 73.1 jit_solution(5902399300299031560)
XLA Ops:
  1.3 69.9 %shard_map.103 = (bf16[128,256]{1,0:T(8,128)(2,1)S(1)}, bf16[128,128]{1,0:T(8,128)(2,1)S(1)}, f32[128,256]{1,0:T(8,128)S(1)}) custom-call(bf16[128,128]{1,0:T(8,128)(2,1)} %features.1, bf16[128,256]{1,0:T(8,128)(2,1)} %weight.1, bf16[144,128,128]{2,1,0:T(8,128)(2,1)} %bitcast.4, s32[1,144]{1,0:T(1,128)} %bitcast.5, s32[1,144]{1,0:T(1,128)} %bitcast.6, ...), custom_call_target="tpu_custom_call" | custom-call | tf_op jit(solution)/shard_map/pallas_call | solution.py:323
  71.2 0.6 copy.15
  71.8 0.6 copy.16
  72.5 0.7 copy.17

commit v4 on v3

--- a/solution.py
+++ b/solution.py
@@ -12,7 +12,7 @@
 RING8 = (4, 3, 5, 2, 6, 1, 7)
 RING4 = (2, 1, 3)
 FORWARD_STEP, BACKWARD_STEP = 20, 22
-HALF = 64
+PARTS = (48, 80)
 BF, F32, I32 = jnp.bfloat16, jnp.float32, jnp.int32
 
 
@@ -64,12 +64,14 @@
 
 def kernel(features, weight, tiles, tile_row, tile_col, labels, cotangent, tile_count,
            act_out, gf_out, gw_out,
-           tile_buf, xbuf, gbuf_a, gbuf_b, pref, pref2, pblk, cr, ystage, yr, bblk, xr, zstage, zr, wbuf, cbuf, slots,
+           tile_buf, xbuf, gbuf_a, gbuf_b, pref, pref_a, pref_b, pblk, cr, ystage, yr, bblk_a, bblk_b, xr_a, xr_b,
+           zstage_a, zstage_b, zr_a, zr_b, wbuf, cbuf, slots,
            plan_v, plan_f, plan_b, wt, w0r, wh, w1r, w2b, w3b, rows_v, cols_v, labels_v,
            loc, ag_s, ag_r, c_s, c_r, y_s, y_r, g_s, g_r, x_s, x_r, z_s, z_r,
            w_s, w0_r, w1_r, w2_r, w3_r, w4_r, w5_r):
     r, c = lax.axis_index("row"), lax.axis_index("col")
-    gbuf = (gbuf_a, gbuf_b)
+    gbuf, pref2, bblk = (gbuf_a, gbuf_b), (pref_a, pref_b), (bblk_a, bblk_b)
+    xr, zstage, zr = (xr_a, xr_b), (zstage_a, zstage_b), (zr_a, zr_b)
     x, z, y, k = r // NZ, r % NZ, c // 2, c % 2
     other = 1 - k
 
@@ -132,7 +134,7 @@
     live = iota((1, WIDE), 1) < tile_count[0, 0]
     xbuf[NX * NZ] = jnp.zeros((T, T), BF)
     for h in range(2):
-        gbuf[h][NY * 2] = jnp.zeros((HALF, T), BF)
+        gbuf[h][NY * 2] = jnp.zeros((PARTS[h], T), BF)
     to_row = ((rows_here // 2 - y + NY) % NY) * 2 + (rows_here + k) % 2
     from_row = ((y - rows_here // 2 + NY) % NY) * 2 + (rows_here + k) % 2
     to_col = ((cols_here // NZ - x + NX) % NX) * NZ + (cols_here - z + NZ) % NZ
@@ -204,14 +206,15 @@
     sigmoid_v = jax.nn.sigmoid(preact)
     grad_pre = (masked * sigmoid_v * (1.0 + preact * (1.0 - sigmoid_v))).astype(BF)
     projected = mm_t(wbuf[...], grad_pre).astype(BF)
-    gbuf[0][0] = projected[:HALF]
-    gbuf[1][0] = projected[HALF:]
-
-    for h in range(2):
+    gbuf[0][0] = projected[:PARTS[0]]
+    gbuf[1][0] = projected[PARTS[0]:]
+
+    def send_y(h):
         for dy in (1, 7, 2, 6, 3, 5, 4):
             push(gbuf[h].at[0], gbuf[h].at[dy * 2], g_s.at[h, dy * 2], g_r.at[h, dy * 2], at_y(dy))
         push(gbuf[h].at[0], gbuf[h].at[1], g_s.at[h, 1], g_r.at[h, 1], sibling)
-    act_out[...] = (preact * sigmoid_v).astype(BF)
+
+    send_y(0)
     wt[...] = lax.dot_general(aggregate, grad_pre, (((0,), (0,)), ((), ())), preferred_element_type=F32)
     half = T // 2
     mine = pl.ds(pl.multiple_of(k * half, half), half)
@@ -226,6 +229,9 @@
 
     for ey in RING8:
         push(wh.at[rows_of(ey)], w1r.at[ey], w_s.at[ey], w1_r.at[ey], at_y(ey))
+    send_y(1)
+    act_out[...] = (preact * sigmoid_v).astype(BF)
+
     def hand_on(h):
         for dy in (1, 7, 2, 6, 3, 5, 4):
             arrived(gbuf[h].at[dy * 2], g_r.at[h, dy * 2])
@@ -234,16 +240,16 @@
     def transposed_sums(h):
         for dy in (0, 1, 7, 2, 6, 3, 5, 4):
             arrived(gbuf[h].at[dy * 2 + 1], g_r.at[h, dy * 2 + 1])
-        run(plan_b, (slots_all + NX * NZ) // 2, BACKWARD_STEP, gbuf[h].shape[0], pref2.at[h], backward(h))
+        run(plan_b, (slots_all + NX * NZ) // 2, BACKWARD_STEP, gbuf[h].shape[0], pref2[h], backward(h))
 
     def send_x(h):
         for ez in RING8 + (0,):
             for ex in RING4:
                 g = ex * NZ + ez
-                bblk[h, g] = result(plan_b, g, pref2.at[h])
-                push(bblk.at[h, g], xr.at[h, g], x_s.at[h, g], x_r.at[h, g], at_x(ex))
+                bblk[h][g] = result(plan_b, g, pref2[h])
+                push(bblk[h].at[g], xr[h].at[g], x_s.at[h, g], x_r.at[h, g], at_x(ex))
         for ez in range(NZ):
-            bblk[h, ez] = result(plan_b, ez, pref2.at[h])
+            bblk[h][ez] = result(plan_b, ez, pref2[h])
 
     hand_on(0)
     transposed_sums(0)
@@ -258,7 +264,6 @@
 
     send_x(0)
     transposed_sums(1)
-    send_x(1)
     for dx in RING4:
         arrived(w2b.at[(x + NX - dx) % NX], w2_r.at[dx])
     term = w2b[0]
@@ -267,13 +272,14 @@
     w3b[z] = term
     for dz in RING8:
         push(w3b.at[z], w3b.at[z], w_s.at[12 + dz], w3_r.at[dz], at_z(dz))
+    send_x(1)
 
     def x_total(h, ez):
-        total = bblk[h, ez].astype(F32)
+        total = bblk[h][ez].astype(F32)
         for ex in (1, 3, 2):
             g = ex * NZ + ez
-            arrived(xr.at[h, g], x_r.at[h, g])
-            total = total + xr[h, g].astype(F32)
+            arrived(xr[h].at[g], x_r.at[h, g])
+            total = total + xr[h][g].astype(F32)
         return total
 
     def gw_rows(d):
@@ -281,8 +287,8 @@
 
     def send_z(h):
         for ez in RING8:
-            zstage[h, ez] = x_total(h, ez).astype(BF)
-            push(zstage.at[h, ez], zr.at[h, ez], z_s.at[h, ez], z_r.at[h, ez], at_z(ez))
+            zstage[h][ez] = x_total(h, ez).astype(BF)
+            push(zstage[h].at[ez], zr[h].at[ez], z_s.at[h, ez], z_r.at[h, ez], at_z(ez))
 
     send_z(0)
     for dz in RING8:
@@ -300,11 +306,11 @@
         arrived(gw_out.at[gw_rows(-dy)], w4_r.at[dy])
     push(gw_out.at[mine], gw_out.at[mine], w_s.at[28], w5_r, sibling)
     for ez in (1, 7, 2, 6, 3, 5, 4):
-        arrived(zr.at[0, ez], z_r.at[0, ez])
-        total_a = total_a + zr[0, ez].astype(F32)
+        arrived(zr[0].at[ez], z_r.at[0, ez])
+        total_a = total_a + zr[0][ez].astype(F32)
     for ez in (1, 7, 2, 6, 3, 5, 4):
-        arrived(zr.at[1, ez], z_r.at[1, ez])
-        total_b = total_b + zr[1, ez].astype(F32)
+        arrived(zr[1].at[ez], z_r.at[1, ez])
+        total_b = total_b + zr[1][ez].astype(F32)
     gf_out[...] = jnp.transpose(jnp.concatenate([total_a, total_b], axis=0)).astype(BF)
     arrived(gw_out.at[theirs], w5_r)
     for copy in sends:
@@ -332,18 +338,17 @@
         scratch_shapes=[
             V((count, T, T), BF),
             V((NX * NZ + 1, T, T), BF),
-            V((NY * 2 + 1, HALF, T), BF),
-            V((NY * 2 + 1, HALF, T), BF),
+            *[V((NY * 2 + 1, p, T), BF) for p in PARTS],
             V(((count + NY * 2) // 2, T, T), F32),
-            V((2, pairs, HALF, T), F32),
+            *[V((pairs, p, T), F32) for p in PARTS],
             V((NY * 2, T, T), BF),
             V((NY, T, T), BF),
             V((NY, T, T), BF),
             V((NY, T, T), BF),
-            V((2, NX * NZ, HALF, T), BF),
-            V((2, NX * NZ, HALF, T), BF),
-            V((2, NZ, HALF, T), BF),
-            V((2, NZ, HALF, T), BF),
+            *[V((NX * NZ, p, T), BF) for p in PARTS],
+            *[V((NX * NZ, p, T), BF) for p in PARTS],
+            *[V((NZ, p, T), BF) for p in PARTS],
+            *[V((NZ, p, T), BF) for p in PARTS],
             V((width, hidden), BF),
             V((nodes, hidden), BF),
             V((8, WIDE), I32),

time: 73.3 us -> 73.1 us (level)
  no operation moved by 1% of the time
where the time goes in v4:
time: 73.1 us; the launch traced here: 73 us
  Pallas kernels  69.8 us (95%)
  local copies, waits for them, and re-layouts  1.9 us (3%)
  between operations  1.29 us (2%)
    pallas_call x1, Pallas kernels, shards(): pl.pallas_call(kernel, out_shape=(jax.ShapeDtypeStruct((nodes, hidden), B...  69.8 us
    unnamed x3, local copies, waits for them, and re-layouts  1.9 us

profile of v4, /device:TPU:1, one launch (start us, length us, event | category | flops | bytes accessed | tf_op | source)
XLA Modules:
  0.0 73.0 jit_solution(14580178209417158263)
XLA Ops:
  1.3 69.8 %shard_map.103 = (bf16[128,256]{1,0:T(8,128)(2,1)S(1)}, bf16[128,128]{1,0:T(8,128)(2,1)S(1)}, f32[128,256]{1,0:T(8,128)S(1)}) custom-call(bf16[128,128]{1,0:T(8,128)(2,1)} %features.1, bf16[128,256]{1,0:T(8,128)(2,1)} %weight.1, bf16[144,128,128]{2,1,0:T(8,128)(2,1)} %bitcast.4, s32[1,144]{1,0:T(1,128)} %bitcast.5, s32[1,144]{1,0:T(1,128)} %bitcast.6, ...), custom_call_target="tpu_custom_call" | custom-call | tf_op jit(solution)/shard_map/pallas_call | solution.py:329
  71.1 0.6 copy.15
  71.7 0.6 copy.16
  72.3 0.7 copy.17
